TPU v7x, 32 devices: a whole 2x2x4 slice. The times are simulated.
32 devices in a mesh: clips: 2 (over y), tm: 4 (over x, core), rows: 4 (over z).
Axes of the slice: x: 2, y: 2, z: 4, core: 2. Of those that a mesh axis runs over, the one named last changes fastest.
Arguments:
- features: bfloat16 [8, 8, 48, 384], P(('clips', 'tm'), 'rows'), parts along dimension 0, may hold values from -320 to 320
- first_gain: float32 [384], replicated, may hold values from 0.5 to 1.5
- first_shift: float32 [384], replicated, may hold values from -3 to 3
- first_kernel: bfloat16 [384, 3, 3, 3, 384], P('tm'), may hold values from -0.0625 to 0.0625
- first_bias: float32 [384], P('tm'), may hold values from -2 to 2
- second_gain: float32 [384], replicated, may hold values from 0.5 to 1.5
- second_shift: float32 [384], replicated, may hold values from -3 to 3
- second_kernel: bfloat16 [384, 3, 3, 3, 384], P('tm'), may hold values from -0.0625 to 0.0625
- second_bias: float32 [384], P('tm'), may hold values from -2 to 2
- third_gain: float32 [384], replicated, may hold values from 0.5 to 1.5
- third_shift: float32 [384], replicated, may hold values from -3 to 3
- query_weight: bfloat16 [384, 384], replicated, may hold values from -0.30618622 to 0.30618622
- key_weight: bfloat16 [384, 384], replicated, may hold values from -1.8371173 to 1.8371173
- value_weight: bfloat16 [384, 384], replicated, may hold values from -0.3125 to 0.3125
- output_weight: bfloat16 [384, 384], replicated, may hold values from -0.3125 to 0.3125
Outputs:
- decoded: bfloat16 [8, 8, 48, 384], P(('clips', 'tm'), 'rows'), parts along dimension 0
There are 2 independent parts, one for each index of `clips`. A program takes and returns all parts, laid end to end along the dimension named above; an argument that names none is the same for every part. Nothing has to cross between parts.
All inputs are finite; a program needn't handle non-finite values.
Results may differ from a plain program's by a relative error of at most 0.029.
Values may be sent and summed in bfloat16 or wider, within the bound.
No kernel may reach another device: no remote copies, remote signals or barrier semaphores. Data moves between devices by JAX's collectives and lax.ppermute only.
A program may use at most 64 MiB of HBM per device.

v0:
```python
import jax
import jax.numpy as jnp
from jax import lax
from jax.sharding import PartitionSpec as P

C = 384
GROUPS = 32


epsilon = 1e-06


def extended(cells, sides, width):
    for axis, dim in sides:
        count = lax.axis_size(axis)
        ends = count - 1
        head = lax.slice_in_dim(cells, 0, width, axis=dim)
        tail = lax.slice_in_dim(cells, cells.shape[dim] - width, cells.shape[dim], axis=dim)
        cells = jnp.concatenate(
            [
                lax.ppermute(tail, axis, [(i, (i + 1) % count) for i in range(ends)]),
                cells,
                lax.ppermute(head, axis, [((i + 1) % count, i) for i in range(ends)]),
            ],
            axis=dim,
        )
    return cells


def group_norm(values, gain, shift):
    frame_count, row_count, col_count, channels = values.shape
    entries = lax.axis_size("rows") * row_count * col_count * (channels // GROUPS)
    grouped = values.reshape(frame_count, row_count, col_count, GROUPS, channels // GROUPS)
    sums = lax.psum(jnp.sum(grouped, axis=(1, 2, 4)), "rows")
    average = sums / entries
    centered = grouped - average[:, None, None, :, None]
    variance = lax.psum(jnp.sum(centered * centered, axis=(1, 2, 4)), "rows") / entries
    scaled = centered * lax.rsqrt(variance + epsilon)[:, None, None, :, None]
    return scaled.reshape(frame_count, row_count, col_count, channels) * gain + shift


def causal_conv(active, kernel, bias):
    widened = extended(active, (("rows", 1),), 1)
    clip_frames = lax.all_gather(widened, "tm", axis=0, tiled=True)
    frame_count, padded_rows, col_count, channels = clip_frames.shape
    row_count = padded_rows - 2
    outputs = kernel.shape[0]
    padded = jnp.pad(clip_frames, ((2, 0), (0, 0), (1, 1), (0, 0)))
    summed = jnp.zeros((outputs, frame_count * row_count * col_count), jnp.float32)
    for tap_time in range(3):
        for tap_row in range(3):
            window = padded[tap_time : tap_time + frame_count, tap_row : tap_row + row_count]
            stacked = jnp.concatenate(
                [window[:, :, shift_col : shift_col + col_count] for shift_col in range(3)], axis=-1
            )
            tap_weight = kernel[:, tap_time, tap_row].reshape(outputs, 3 * channels)
            summed = summed + lax.dot_general(
                tap_weight,
                stacked.reshape(-1, 3 * channels),
                (((1,), (1,)), ((), ())),
                preferred_element_type=jnp.float32,
            )
    result = (
        (summed + bias[:, None])
        .astype(jnp.bfloat16)
        .reshape(outputs, frame_count, row_count, col_count)
    )
    mixed = lax.all_to_all(result, "tm", split_axis=1, concat_axis=0, tiled=True)
    return jnp.transpose(mixed, (1, 2, 3, 0))


def absorb(carry, queries, keys, values):
    peak, total, summed = carry
    scores = jnp.einsum("fqc,fkc->fqk", queries, keys, preferred_element_type=jnp.float32)
    new_peak = jnp.max(scores, axis=-1)
    factor = jnp.exp(peak - new_peak)
    expon = jnp.exp(scores - new_peak[..., None])
    total = total * factor + jnp.sum(expon, axis=-1)
    summed = summed * factor[..., None] + jnp.einsum(
        "fqk,fkc->fqc", expon.astype(jnp.bfloat16), values, preferred_element_type=jnp.float32
    )
    return (new_peak, total, summed)


def per_device(
    features,
    first_gain,
    first_shift,
    first_kernel,
    first_bias,
    second_gain,
    second_shift,
    second_kernel,
    second_bias,
    third_gain,
    third_shift,
    query_weight,
    key_weight,
    value_weight,
    output_weight,
):
    frame_count, row_count, col_count, channels = features.shape
    start = features.astype(jnp.float32)
    active1 = jax.nn.silu(group_norm(start, first_gain, first_shift)).astype(jnp.bfloat16)
    conv1 = causal_conv(active1, first_kernel, first_bias)
    active2 = jax.nn.silu(group_norm(conv1.astype(jnp.float32), second_gain, second_shift)).astype(
        jnp.bfloat16
    )
    conv2 = causal_conv(active2, second_kernel, second_bias)
    hidden = (start + conv2.astype(jnp.float32)).astype(jnp.bfloat16)
    normed = group_norm(hidden.astype(jnp.float32), third_gain, third_shift).astype(jnp.bfloat16)
    flat = normed.reshape(frame_count, row_count * col_count, channels)
    queries = (
        jnp.einsum("fpc,cd->fpd", flat, query_weight, preferred_element_type=jnp.float32)
        * C ** (-0.5)
    ).astype(jnp.bfloat16)
    positions = row_count * col_count
    initial = (
        jnp.full((frame_count, positions), -jnp.inf, jnp.float32),
        jnp.zeros((frame_count, positions), jnp.float32),
        jnp.zeros((frame_count, positions, channels), jnp.float32),
    )
    keys = jnp.einsum("fpc,cd->fpd", flat, key_weight, preferred_element_type=jnp.float32).astype(
        jnp.bfloat16
    )
    values = jnp.einsum(
        "fpc,cd->fpd", flat, value_weight, preferred_element_type=jnp.float32
    ).astype(jnp.bfloat16)
    shape4 = (frame_count, row_count, col_count, channels)
    peak, total, summed = absorb(
        initial,
        queries,
        lax.all_gather(keys.reshape(shape4), "rows", axis=1, tiled=True).reshape(
            frame_count, -1, channels
        ),
        lax.all_gather(values.reshape(shape4), "rows", axis=1, tiled=True).reshape(
            frame_count, -1, channels
        ),
    )
    attended = (summed / total[..., None]).astype(jnp.bfloat16)
    projected = jnp.einsum(
        "fpc,cd->fpd", attended, output_weight, preferred_element_type=jnp.float32
    )
    decoded = hidden.astype(jnp.float32) + projected.reshape(
        frame_count, row_count, col_count, channels
    )
    return decoded.astype(jnp.bfloat16)


def solution(mesh):
    in_specs = (
        P(("clips", "tm"), "rows", None, None),
        P(),
        P(),
        P("tm", None, None, None, None),
        P("tm"),
        P(),
        P(),
        P("tm", None, None, None, None),
        P("tm"),
        P(),
        P(),
        P(),
        P(),
        P(),
        P(),
    )
    out_specs = P(("clips", "tm"), "rows", None, None)
    return jax.shard_map(
        per_device, mesh=mesh, in_specs=in_specs, out_specs=out_specs, check_vma=False
    )
```

profile of v0, /device:TPU:0, one launch (start us, length us, event | category | flops | bytes accessed | tf_op | source)
XLA Modules:
  0.0 157.3 jit_solution(10581170224222182222)
XLA Ops:
  0.0 1.0 convert_reduce_fusion.1
  1.2 13.5 %psum.42 = f32[1,32]{1,0:T(1,128)S(1)} all-reduce(f32[1,32]{1,0:T(1,128)S(1)} %bitcast.277), channel_id=1, replica_groups=mesh['clips'=2,'tm'=4,'rows'=4] {'rows'}, use_global_device_ids=true, to_apply=%region_2.0 | all-reduce | flops 32 | bytes 256 | tf_op jit(solution)/shard_map/psum | solution.py:34
  14.8 0.9 fusion.21
  16.0 8.4 %psum.43 = f32[1,32]{1,0:T(1,128)S(1)} all-reduce(f32[1,32]{1,0:T(1,128)S(1)} %bitcast.278), channel_id=1, replica_groups=mesh['clips'=2,'tm'=4,'rows'=4] {'rows'}, use_global_device_ids=true, to_apply=%region_5.6 | all-reduce | flops 32 | bytes 256 | tf_op jit(solution)/shard_map/psum | solution.py:37
  24.5 1.0 fusion.29
  25.5 3.9 %collective-permute-start = (bf16[1,1,48,384]{3,2,1,0:T(8,128)(2,1)S(1)}, bf16[1,1,48,384]{3,2,1,0:T(8,128)(2,1)S(1)}, u32[]{:S(2)}, u32[]{:S(2)}) collective-permute-start(bf16[1,1,48,384]{3,2,1,0:T(8,128)(2,1)S(1)} %get-tuple-element.81), channel_id=1, source_target_pairs={{0,1},{1,2},{2,3},{4,5},{5,6},{6,7},{8,9},{9,10},{10,11},{12,13},{... | collective-permute-start | bytes 110600 | tf_op jit(solution)/shard_map/ppermute | solution.py:21
  29.4 1.3 collective-permute-start.1
  30.7 1.8 %fusion.45 = (bf16[96,1,1,3,384]{4,0,3,2,1:T(8,128)(2,1)S(1)}, bf16[96,1,1,3,384]{4,0,3,2,1:T(8,128)(2,1)S(1)}, bf16[96,1,1,3,384]{4,0,3,2,1:T(8,128)(2,1)S(1)},...) fusion(bf16[96,3,3,3,384]{4,0,3,2,1:T(8,128)(2,1)} %param.18), kind=kLoop, calls=%fused_computation.150 | loop fusion | bytes 3981312 | tf_op jit(solution)/shard_map/slice | solution.py:56
  34.3 1.0 collective-permute-done.1
  35.3 7.5 %all_gather.12 = bf16[4,4,48,384]{3,2,1,0:T(8,128)(2,1)S(1)} all-gather(bf16[1,4,48,384]{3,2,1,0:T(8,128)(2,1)S(1)} %pad_maximum_fusion.18), channel_id=1, replica_groups=mesh['clips'=2,'tm'=4,'rows'=4] {'tm'}, dimensions={0}, use_global_device_ids=true | all-gather | bytes 737280 | tf_op jit(solution)/shard_map/all_gather | solution.py:44
  42.8 1.8 %pad_slice_fusion.25 = (bf16[4,2,48,384]{3,2,1,0:T(8,128)(2,1)S(1)}, bf16[4,2,48,384]{3,2,1,0:T(8,128)(2,1)S(1)}, bf16[4,2,48,384]{3,2,1,0:T(8,128)(2,1)S(1)}, b...) fusion(bf16[4,4,48,384]{3,2,1,0:T(8,128)(2,1)S(1)} %all_gather.12), kind=kLoop, calls=%fused_computation.25 | loop fusion | bytes 6193152 | tf_op jit(solution)/shard_map/slice | solution.py:54
  44.6 0.3 fusion.47
  45.1 0.4 fusion.51
  45.5 0.4 convolution_add_fusion.16
  46.1 0.4 convolution_add_fusion.15
  46.5 0.4 convolution_add_fusion.14
  47.1 0.4 convolution_add_fusion.13
  47.5 0.4 convolution_add_fusion.12
  48.1 0.4 convolution_add_fusion.11
  48.6 0.4 convolution_add_fusion.10
  49.2 0.4 fusion.10
  49.7 6.7 %all_to_all.8 = bf16[96,4,2,48]{0,3,2,1:T(8,128)(2,1)S(1)} all-to-all(bf16[96,4,2,48]{0,3,2,1:T(8,128)(2,1)S(1)} %bitcast.270), channel_id=1, replica_groups=mesh['clips'=2,'tm'=4,'rows'=4] {'tm'}, dimensions={1} | all-to-all | bytes 147456 | tf_op jit(solution)/shard_map/all_to_all | solution.py:68
  56.9 10.1 %psum.44 = f32[1,32]{1,0:T(1,128)S(1)} all-reduce(f32[1,32]{1,0:T(1,128)S(1)} %bitcast.279), channel_id=1, replica_groups=mesh['clips'=2,'tm'=4,'rows'=4] {'rows'}, use_global_device_ids=true, to_apply=%region_8.9 | all-reduce | flops 32 | bytes 256 | tf_op jit(solution)/shard_map/psum | solution.py:34
  67.5 8.7 %psum.45 = f32[1,32]{1,0:T(1,128)S(1)} all-reduce(f32[1,32]{1,0:T(1,128)S(1)} %bitcast.280), channel_id=1, replica_groups=mesh['clips'=2,'tm'=4,'rows'=4] {'rows'}, use_global_device_ids=true, to_apply=%region_11.12 | all-reduce | flops 32 | bytes 256 | tf_op jit(solution)/shard_map/psum | solution.py:37
  76.4 3.6 %collective-permute-start.2 = (bf16[1,1,48,384]{3,2,1,0:T(8,128)(2,1)S(1)}, bf16[1,1,48,384]{3,2,1,0:T(8,128)(2,1)S(1)}, u32[]{:S(2)}, u32[]{:S(2)}) collective-permute-start(bf16[1,1,48,384]{3,2,1,0:T(8,128)(2,1)S(1)} %get-tuple-element.79), channel_id=1, source_target_pairs={{0,1},{1,2},{2,3},{4,5},{5,6},{6,7},{8,9},{9,10},{10,11},{12,13},{... | collective-permute-start | bytes 110600 | tf_op jit(solution)/shard_map/ppermute | solution.py:21
  80.0 1.3 collective-permute-start.3
  81.3 0.2 fusion.44
  83.3 2.5 %collective-permute-done.3 = bf16[1,1,48,384]{3,2,1,0:T(8,128)(2,1)S(1)} collective-permute-done((bf16[1,1,48,384]{3,2,1,0:T(8,128)(2,1)S(1)}, bf16[1,1,48,384]{3,2,1,0:T(8,128)(2,1)S(1)}, u32[]{:S(2)}, u32[]{:S(2)}) %collective-permute-start.3) | collective-permute-done | bytes 36896 | tf_op jit(solution)/shard_map/ppermute | solution.py:23
  85.9 6.9 %all_gather.13 = bf16[4,4,48,384]{3,2,1,0:T(8,128)(2,1)S(1)} all-gather(bf16[1,4,48,384]{3,2,1,0:T(8,128)(2,1)S(1)} %pad_maximum_fusion.19), channel_id=1, replica_groups=mesh['clips'=2,'tm'=4,'rows'=4] {'tm'}, dimensions={0}, use_global_device_ids=true | all-gather | bytes 737280 | tf_op jit(solution)/shard_map/all_gather | solution.py:44
  92.8 1.7 %pad_slice_fusion.1 = (bf16[4,2,48,384]{3,2,1,0:T(8,128)(2,1)S(1)}, bf16[4,2,48,384]{3,2,1,0:T(8,128)(2,1)S(1)}, bf16[4,2,48,384]{3,2,1,0:T(8,128)(2,1)S(1)}, bf...) fusion(bf16[4,4,48,384]{3,2,1,0:T(8,128)(2,1)S(1)} %all_gather.13), kind=kLoop, calls=%fused_computation.1 | loop fusion | bytes 6193152 | tf_op jit(solution)/shard_map/slice | solution.py:54
  94.5 0.3 fusion.46
  94.9 0.4 fusion.52
  96.0 0.4 convolution_add_fusion.8
  96.5 0.4 convolution_add_fusion.7
  96.9 0.4 convolution_add_fusion.6
  97.3 0.4 convolution_add_fusion.5
  97.7 0.4 convolution_add_fusion.4
  98.1 0.4 convolution_add_fusion.3
  98.5 0.4 convolution_add_fusion.2
  99.0 0.4 fusion.11
  99.5 6.7 %all_to_all.9 = bf16[96,4,2,48]{0,3,2,1:T(8,128)(2,1)S(1)} all-to-all(bf16[96,4,2,48]{0,3,2,1:T(8,128)(2,1)S(1)} %bitcast.271), channel_id=1, replica_groups=mesh['clips'=2,'tm'=4,'rows'=4] {'tm'}, dimensions={1} | all-to-all | bytes 147456 | tf_op jit(solution)/shard_map/all_to_all | solution.py:68
  106.8 8.5 %psum.46 = f32[1,32]{1,0:T(1,128)S(1)} all-reduce(f32[1,32]{1,0:T(1,128)S(1)} %bitcast.281), channel_id=1, replica_groups=mesh['clips'=2,'tm'=4,'rows'=4] {'rows'}, use_global_device_ids=true, to_apply=%region_14.15 | all-reduce | flops 32 | bytes 256 | tf_op jit(solution)/shard_map/psum | solution.py:34
  115.8 10.2 %psum.47 = f32[1,32]{1,0:T(1,128)S(1)} all-reduce(f32[1,32]{1,0:T(1,128)S(1)} %bitcast.276), channel_id=1, replica_groups=mesh['clips'=2,'tm'=4,'rows'=4] {'rows'}, use_global_device_ids=true, to_apply=%region_17.18 | all-reduce | flops 32 | bytes 256 | tf_op jit(solution)/shard_map/psum | solution.py:37
  126.5 14.7 %all_gather.14 = bf16[1,8,48,384]{3,2,0,1:T(8,128)(2,1)S(1)} all-gather(bf16[1,2,48,384]{3,2,0,1:T(8,128)(2,1)S(1)} %bitcast.274), channel_id=1, replica_groups=mesh['clips'=2,'tm'=4,'rows'=4] {'rows'}, dimensions={1}, use_global_device_ids=true | all-gather | bytes 368640 | tf_op jit(solution)/shard_map/all_gather | solution.py:133
  141.2 0.5 fusion.50
  142.1 14.1 %all_gather.15 = bf16[1,8,48,384]{3,2,0,1:T(8,128)(2,1)S(1)} all-gather(bf16[1,2,48,384]{3,2,0,1:T(8,128)(2,1)S(1)} %bitcast.273), channel_id=1, replica_groups=mesh['clips'=2,'tm'=4,'rows'=4] {'rows'}, dimensions={1}, use_global_device_ids=true | all-gather | bytes 368640 | tf_op jit(solution)/shard_map/all_gather | solution.py:136
  156.2 0.3 fusion.8
  156.4 0.8 fusion.4
  (128 shorter events, 9.0 us)
Async XLA Ops:
  0.0 141.2 %copy-start = (bf16[384,384]{1,0:T(8,128)(2,1)S(1)}, bf16[384,384]{1,0:T(8,128)(2,1)}, u32[]{:S(2)}) copy-start(bf16[384,384]{1,0:T(8,128)(2,1)} %param.26) | copy-start | bytes 884740
  25.5 8.8 %collective-permute-start = (bf16[1,1,48,384]{3,2,1,0:T(8,128)(2,1)S(1)}, bf16[1,1,48,384]{3,2,1,0:T(8,128)(2,1)S(1)}, u32[]{:S(2)}, u32[]{:S(2)}) collective-permute-start(bf16[1,1,48,384]{3,2,1,0:T(8,128)(2,1)S(1)} %get-tuple-element.81), channel_id=1, source_target_pairs={{0,1},{1,2},{2,3},{4,5},{5,6},{6,7},{8,9},{9,10},{10,11},{12,13},{... | collective-permute-start | bytes 110600 | tf_op jit(solution)/shard_map/ppermute | solution.py:21
  29.4 5.9 %collective-permute-start.1 = (bf16[1,1,48,384]{3,2,1,0:T(8,128)(2,1)S(1)}, bf16[1,1,48,384]{3,2,1,0:T(8,128)(2,1)S(1)}, u32[]{:S(2)}, u32[]{:S(2)}) collective-permute-start(bf16[1,1,48,384]{3,2,1,0:T(8,128)(2,1)S(1)} %get-tuple-element.82), channel_id=1, source_target_pairs={{1,0},{2,1},{3,2},{5,4},{6,5},{7,6},{9,8},{10,9},{11,10},{13,12},{... | collective-permute-start | bytes 110600 | tf_op jit(solution)/shard_map/ppermute | solution.py:23
  48.5 0.7 copy-start.10
  49.0 27.3 %copy-start.6 = (f32[384]{0:T(512)S(1)}, f32[384]{0:T(512)}, u32[]{:S(2)}) copy-start(f32[384]{0:T(512)} %param.21) | copy-start | bytes 4612
  49.0 27.3 %copy-start.7 = (f32[384]{0:T(512)S(1)}, f32[384]{0:T(512)}, u32[]{:S(2)}) copy-start(f32[384]{0:T(512)} %param.20) | copy-start | bytes 4612
  49.0 32.3 %copy-start.1 = (bf16[96,3,3,3,384]{4,0,3,2,1:T(8,128)(2,1)S(1)}, bf16[96,3,3,3,384]{4,0,3,2,1:T(8,128)(2,1)}, u32[]{:S(2)}) copy-start(bf16[96,3,3,3,384]{4,0,3,2,1:T(8,128)(2,1)} %param.22) | copy-start | bytes 5971972
  76.4 6.9 %collective-permute-start.2 = (bf16[1,1,48,384]{3,2,1,0:T(8,128)(2,1)S(1)}, bf16[1,1,48,384]{3,2,1,0:T(8,128)(2,1)S(1)}, u32[]{:S(2)}, u32[]{:S(2)}) collective-permute-start(bf16[1,1,48,384]{3,2,1,0:T(8,128)(2,1)S(1)} %get-tuple-element.79), channel_id=1, source_target_pairs={{0,1},{1,2},{2,3},{4,5},{5,6},{6,7},{8,9},{9,10},{10,11},{12,13},{... | collective-permute-start | bytes 110600 | tf_op jit(solution)/shard_map/ppermute | solution.py:21
  80.0 5.9 %collective-permute-start.3 = (bf16[1,1,48,384]{3,2,1,0:T(8,128)(2,1)S(1)}, bf16[1,1,48,384]{3,2,1,0:T(8,128)(2,1)S(1)}, u32[]{:S(2)}, u32[]{:S(2)}) collective-permute-start(bf16[1,1,48,384]{3,2,1,0:T(8,128)(2,1)S(1)} %get-tuple-element.80), channel_id=1, source_target_pairs={{1,0},{2,1},{3,2},{5,4},{6,5},{7,6},{9,8},{10,9},{11,10},{13,12},{... | collective-permute-start | bytes 110600 | tf_op jit(solution)/shard_map/ppermute | solution.py:23
  97.7 1.3 copy-start.11
  98.5 8.1 %copy-start.2 = (bf16[1,2,48,384]{3,2,1,0:T(8,128)(2,1)S(1)}, bf16[1,2,48,384]{3,2,1,0:T(8,128)(2,1)}, u32[]{:S(2)}) copy-start(bf16[1,2,48,384]{3,2,1,0:T(8,128)(2,1)} %param.15) | copy-start | bytes 221188
  98.9 27.3 %copy-start.8 = (f32[384]{0:T(512)S(1)}, f32[384]{0:T(512)}, u32[]{:S(2)}) copy-start(f32[384]{0:T(512)} %param.25) | copy-start | bytes 4612
  99.0 27.3 %copy-start.9 = (f32[384]{0:T(512)S(1)}, f32[384]{0:T(512)}, u32[]{:S(2)}) copy-start(f32[384]{0:T(512)} %param.24) | copy-start | bytes 4612
  99.0 27.4 %copy-start.3 = (bf16[384,384]{1,0:T(8,128)(2,1)S(1)}, bf16[384,384]{1,0:T(8,128)(2,1)}, u32[]{:S(2)}) copy-start(bf16[384,384]{1,0:T(8,128)(2,1)} %param.27) | copy-start | bytes 884740
  106.3 35.6 %copy-start.4 = (bf16[384,384]{1,0:T(8,128)(2,1)S(1)}, bf16[384,384]{1,0:T(8,128)(2,1)}, u32[]{:S(2)}) copy-start(bf16[384,384]{1,0:T(8,128)(2,1)} %param.28) | copy-start | bytes 884740
  126.3 30.1 %copy-start.5 = (bf16[384,384]{1,0:T(8,128)(2,1)S(1)}, bf16[384,384]{1,0:T(8,128)(2,1)}, u32[]{:S(2)}) copy-start(bf16[384,384]{1,0:T(8,128)(2,1)} %param.29) | copy-start | bytes 884740
where the time goes:
time: 158 us; the launch traced here: 157 us
  blocking collectives  116 us (73%)
  local copies, waits for them, and re-layouts  12.1 us (8%)
  starting transfers between devices  10.1 us (6%)
  matrix products  9.27 us (6%)
  other arithmetic  5.53 us (4%)
  waiting for transfers between devices  3.52 us (2%)
    psum x3, blocking collectives, group_norm(): sums = lax.psum(jnp.sum(grouped, axis=(1, 2, 4)), 'rows')  32.1 us
    psum x3, blocking collectives, group_norm(): lax.psum(jnp.sum(centered * centered, axis=(1, 2, 4)), 'rows') / entries  27.3 us
    all_gather x1, blocking collectives, per_device(): lax.all_gather(keys.reshape(shape4), 'rows', axis=1, tiled=True)  14.7 us
    all_gather x2, blocking collectives, causal_conv(): clip_frames = lax.all_gather(widened, 'tm', axis=0, tiled=True)  14.4 us
    all_gather x1, blocking collectives, per_device(): lax.all_gather(values.reshape(shape4), 'rows', axis=1, tiled=True)  14.1 us
    all_to_all x2, blocking collectives, causal_conv(): lax.all_to_all(result, 'tm', split_axis=1, concat_axis=0, tiled=True)  13.4 us
    ppermute x2, starting transfers between devices, extended(): lax.ppermute(tail, axis, [(i, (i + 1) % count) for i in range(ends)])  7.47 us
    dot_general x18, matrix products, causal_conv(): lax.dot_general(tap_weight, stacked.reshape(-1, 3 * channels), (((1,), (1...  7.32 us
  transfers between devices with their start and end apart: 4, of which 2 were waited for; matrix products, arithmetic and copies ran while one was open for 3% of the time, Pallas kernels for 0%

commit v1 on v0

v1 whole, which is shorter than its diff:
```python
import functools

import jax
import jax.numpy as jnp
from jax import lax
from jax.experimental import pallas as pl
from jax.experimental.pallas import tpu as pltpu
from jax.sharding import PartitionSpec as P

C = 384
GROUPS = 32
GROUP = C // GROUPS
EPSILON = 1e-06
VMEM = pl.BlockSpec(memory_space=pltpu.VMEM)
SMEM = pl.BlockSpec(memory_space=pltpu.SMEM)
F32 = jnp.float32
BF16 = jnp.bfloat16


def call(body, outs, scratch=(), **kwargs):
    def run(*args):
        return pl.pallas_call(
            body,
            out_shape=outs,
            in_specs=[SMEM if a.dtype == jnp.int32 else VMEM for a in args],
            out_specs=jax.tree.map(lambda _: VMEM, outs),
            scratch_shapes=scratch,
            compiler_params=pltpu.CompilerParams(vmem_limit_bytes=40 * 1024 * 1024),
            **kwargs,
        )(*args)

    return run


def struct(shape, dtype=BF16):
    return jax.ShapeDtypeStruct(shape, dtype)


def group_sums(rows):
    channels = rows.shape[-1]
    first = lax.broadcasted_iota(jnp.int32, (channels, channels), 0)
    second = lax.broadcasted_iota(jnp.int32, (channels, channels), 1)
    same = ((first * 43691) >> 19) == ((second * 43691) >> 19)
    return lax.dot_general(
        rows,
        same.astype(F32),
        (((1,), (0,)), ((), ())),
        precision=lax.Precision.HIGHEST,
        preferred_element_type=F32,
    )


def split3(value):
    high = value.astype(BF16).astype(F32)
    rest = value - high
    middle = rest.astype(BF16).astype(F32)
    return high, middle, (rest - middle).astype(BF16).astype(F32)


def merge(means, squares, count):
    mean = sum(means) / len(means)
    spread = sum(jnp.square(m - mean) for m in means)
    return mean, (sum(squares) + count * spread) / (count * len(means))


def silu(value):
    return value / (1.0 + jnp.exp(-value))


def first_stats(x_ref, down_ref, up_ref, own_ref):
    _, rows, cols, channels = x_ref.shape
    x = x_ref[0].astype(F32).reshape(rows * cols, channels)
    count = rows * cols * GROUP
    mean = group_sums(jnp.broadcast_to(jnp.sum(x, axis=0, keepdims=True), (8, channels)))[0:1] / count
    square = group_sums(
        jnp.broadcast_to(jnp.sum(jnp.square(x - mean), axis=0, keepdims=True), (8, channels))
    )[0:1]
    at = lax.broadcasted_iota(jnp.int32, (16, channels), 0)
    block = jnp.zeros((16, channels), F32)
    for i, term in enumerate(split3(mean) + split3(square)):
        block = jnp.where(at == i, term, block)
    block = block.astype(BF16)
    own_ref[...] = block
    down_ref[0:cols] = x_ref[0, rows - 1]
    down_ref[cols : cols + 16] = block
    up_ref[0:cols] = x_ref[0, 0]
    up_ref[cols : cols + 16] = block


def first_norm(n, r_ref, x_ref, prev_ref, next_ref, own_ref, others_ref, gain_ref, shift_ref, out_ref):
    _, rows, cols, channels = x_ref.shape
    blocks = [own_ref[...].astype(F32)]
    if n == 4:
        blocks += [prev_ref[cols : cols + 16].astype(F32), next_ref[cols : cols + 16].astype(F32)]
        blocks += [others_ref[...].astype(F32)]
    else:
        blocks = [others_ref[i].astype(F32) for i in range(n)]
    means = [b[0:1] + b[1:2] + b[2:3] for b in blocks]
    squares = [b[3:4] + b[4:5] + b[5:6] for b in blocks]
    mean, variance = merge(means, squares, rows * cols * GROUP)
    scale = lax.rsqrt(variance + EPSILON) * gain_ref[...]
    shift = shift_ref[...]
    r = r_ref[0]

    def active(v):
        return silu((v.astype(F32) - mean) * scale + shift)

    out_ref[0, 0] = jnp.where(r > 0, active(prev_ref[0:cols]), 0.0).astype(BF16)
    for row in range(rows):
        out_ref[0, 1 + row] = active(x_ref[0, row]).astype(BF16)
    out_ref[0, 1 + rows] = jnp.where(r < n - 1, active(next_ref[0:cols]), 0.0).astype(BF16)


def conv(a_ref, w_ref, bias):
    frames, padded, cols, channels = a_ref.shape
    rows = padded - 2
    outputs = w_ref.shape[2] // 3
    plane = rows * cols
    total = None
    for i in (2, 1, 0):
        count = frames - (2 - i)
        window = jnp.concatenate(
            [a_ref[0:count, j : j + rows].reshape(count * plane, channels) for j in range(3)], axis=1
        )
        weight = jnp.concatenate([w_ref[i, j] for j in range(3)], axis=1)
        term = lax.dot_general(window, weight, (((1,), (1,)), ((), ())), preferred_element_type=F32)
        if total is None:
            total = term
        else:
            head = (frames - count) * plane
            total = jnp.concatenate([total[:head], total[head:] + term], axis=0)
    col = lax.broadcasted_iota(jnp.int32, (frames * rows, cols, outputs), 1).reshape(frames * plane, outputs)
    left = pltpu.roll(total[:, 0:outputs], 1, 0)
    right = pltpu.roll(total[:, 2 * outputs :], frames * plane - 1, 0)
    result = total[:, outputs : 2 * outputs]
    result = result + jnp.where(col > 0, left, 0.0) + jnp.where(col < cols - 1, right, 0.0)
    return (result + bias).astype(BF16)


def first_conv(a_ref, w_ref, bias_ref, out_ref, down_ref, up_ref, own_ref, rows8):
    frames, padded, cols, channels = a_ref.shape
    rows = padded - 2
    outputs = w_ref.shape[2] // 3
    plane = rows * cols
    result = conv(a_ref, w_ref, bias_ref[...])
    out_ref[...] = result.reshape(frames, rows, cols, outputs)
    wide = result.astype(F32).reshape(frames, plane, outputs)
    rows8[...] = jnp.zeros(rows8.shape, F32)
    for f in range(frames):
        rows8[f : f + 1] = jnp.sum(wide[f], axis=0, keepdims=True)
    mean = group_sums(rows8[...]) / (plane * GROUP)
    for f in range(frames):
        rows8[f : f + 1] = jnp.sum(jnp.square(wide[f] - mean[f : f + 1]), axis=0, keepdims=True)
    square = group_sums(rows8[...])
    block = jnp.concatenate(split3(mean) + split3(square), axis=0).astype(BF16)
    size = block.shape[0]
    own_ref[...] = block
    for f in range(frames):
        down_ref[f * cols : (f + 1) * cols] = out_ref[f, rows - 1]
        up_ref[f * cols : (f + 1) * cols] = out_ref[f, 0]
    down_ref[frames * cols : frames * cols + size] = block
    up_ref[frames * cols : frames * cols + size] = block


def second_norm(n, r_ref, x_ref, prev_ref, next_ref, own_ref, others_ref, gain_ref, shift_ref, out_ref):
    frames, rows, cols, channels = x_ref.shape
    step = 8 * (-(-frames // 8))
    size = 6 * step
    base = frames * cols
    blocks = [own_ref[...].astype(F32)]
    if n == 4:
        blocks += [prev_ref[base : base + size].astype(F32), next_ref[base : base + size].astype(F32)]
        blocks += [others_ref[...].astype(F32)]
    else:
        blocks = [others_ref[i].astype(F32) for i in range(n)]
    parts = [[b[q * step : (q + 1) * step] for q in range(6)] for b in blocks]
    means = [p[0] + p[1] + p[2] for p in parts]
    squares = [p[3] + p[4] + p[5] for p in parts]
    mean, variance = merge(means, squares, rows * cols * GROUP)
    scale = lax.rsqrt(variance + EPSILON) * gain_ref[...]
    shift = shift_ref[...]
    r = r_ref[0]
    for f in range(frames):

        def active(v):
            return silu((v.astype(F32) - mean[f : f + 1]) * scale[f : f + 1] + shift)

        out_ref[f, 0] = jnp.where(r > 0, active(prev_ref[f * cols : (f + 1) * cols]), 0.0).astype(BF16)
        for row in range(rows):
            out_ref[f, 1 + row] = active(x_ref[f, row]).astype(BF16)
        out_ref[f, 1 + rows] = jnp.where(r < n - 1, active(next_ref[f * cols : (f + 1) * cols]), 0.0).astype(BF16)


def second_conv(parts_ref, w_ref, bias_ref, out_ref, a_ref):
    count, frames, padded, cols, part = parts_ref.shape
    for f in range(frames):
        for row in range(padded):
            a_ref[f, row] = jnp.concatenate([parts_ref[m, f, row] for m in range(count)], axis=1)
    result = conv(a_ref, w_ref, bias_ref[...])
    out_ref[...] = result.reshape(out_ref.shape)


def add_hidden(x_ref, parts_ref, out_ref):
    _, rows, cols, channels = x_ref.shape
    count = parts_ref.shape[0]
    update = jnp.concatenate([parts_ref[m].astype(F32) for m in range(count)], axis=1)
    out_ref[...] = (x_ref[0].reshape(rows * cols, channels).astype(F32) + update).astype(BF16)


def attention(own_ref, *refs):
    others, (gain_ref, shift_ref, wq_ref, wk_ref, wv_ref, wo_ref, out_ref) = refs[:-7], refs[-7:]
    channels = own_ref.shape[-1]
    own = own_ref[...].astype(F32)
    blocks = [o[...].reshape(-1, channels).astype(F32) for o in others]
    wide = blocks[0] if len(blocks) == 1 else jnp.concatenate([own] + blocks, axis=0)
    positions = wide.shape[0]
    count = positions * GROUP
    mean = group_sums(jnp.broadcast_to(jnp.sum(wide, axis=0, keepdims=True), (8, channels)))[0:1] / count
    centered = wide - mean
    variance = (
        group_sums(jnp.broadcast_to(jnp.sum(centered * centered, axis=0, keepdims=True), (8, channels)))[0:1]
        / count
    )
    scale = lax.rsqrt(variance + EPSILON) * gain_ref[...]
    normed = (centered * scale + shift_ref[...]).astype(BF16)
    mine = ((own - mean) * scale + shift_ref[...]).astype(BF16)
    dot = functools.partial(jnp.dot, preferred_element_type=F32)
    queries = (dot(mine, wq_ref[...]) * C ** (-0.5)).astype(BF16)
    keys = dot(normed, wk_ref[...]).astype(BF16)
    values = dot(normed, wv_ref[...]).astype(BF16)
    scores = lax.dot_general(queries, keys, (((1,), (1,)), ((), ())), preferred_element_type=F32)
    peak = jnp.max(scores, axis=-1, keepdims=True)
    weights = jnp.exp(scores - peak)
    total = jnp.sum(weights, axis=-1, keepdims=True)
    attended = (dot(weights.astype(BF16), values) / total).astype(BF16)
    out_ref[...] = (own + dot(attended, wo_ref[...])).astype(BF16)


def shifted(value, by):
    count = lax.axis_size("rows")
    return lax.ppermute(value, "rows", [(i, (i + by) % count) for i in range(count)])


def around(down, up, own):
    prev, after = shifted(down, 1), shifted(up, -1)
    if lax.axis_size("rows") == 4:
        return prev, after, shifted(own, 2)
    return prev, after, lax.all_gather(own, "rows")


def per_device(
    features,
    first_gain,
    first_shift,
    first_kernel,
    first_bias,
    second_gain,
    second_shift,
    second_kernel,
    second_bias,
    third_gain,
    third_shift,
    query_weight,
    key_weight,
    value_weight,
    output_weight,
):
    _, rows, cols, channels = features.shape
    n, frames = lax.axis_size("rows"), lax.axis_size("tm")
    outputs = first_kernel.shape[0]
    plane = rows * cols
    r = lax.axis_index("rows").astype(jnp.int32).reshape(1)
    start = lax.axis_index("tm") * outputs

    def taps(kernel):
        return jnp.transpose(kernel, (1, 2, 3, 0, 4)).reshape(3, 3, 3 * outputs, channels)

    message = struct((cols + 16, channels))
    down, up, own = call(first_stats, (message, message, struct((16, channels))))(features)
    prev, after, others = around(down, up, own)
    active1 = call(functools.partial(first_norm, n), struct((1, rows + 2, cols, channels)))(
        r, features, prev, after, own, others, first_gain.reshape(1, -1), first_shift.reshape(1, -1)
    )
    clip = lax.all_gather(active1, "tm", axis=0, tiled=True)

    step = 8 * (-(-frames // 8))
    size = 6 * step
    message = struct((frames * cols + size, outputs))
    conv1, down, up, own = call(
        first_conv,
        (struct((frames, rows, cols, outputs)), message, message, struct((size, outputs))),
        (pltpu.VMEM((step, outputs), F32),),
    )(clip, taps(first_kernel), first_bias.reshape(1, -1))
    prev, after, others = around(down, up, own)
    active2 = call(functools.partial(second_norm, n), struct((frames, rows + 2, cols, outputs)))(
        r,
        conv1,
        prev,
        after,
        own,
        others,
        lax.dynamic_slice_in_dim(second_gain, start, outputs).reshape(1, -1),
        lax.dynamic_slice_in_dim(second_shift, start, outputs).reshape(1, -1),
    )
    parts = lax.all_gather(active2, "tm")
    conv2 = call(
        second_conv,
        struct((frames, plane, outputs)),
        (pltpu.VMEM((frames, rows + 2, cols, channels), BF16),),
    )(parts, taps(second_kernel), second_bias.reshape(1, -1))
    mixed = lax.all_to_all(conv2, "tm", split_axis=0, concat_axis=0, tiled=True)
    hidden = call(add_hidden, struct((plane, channels)))(features, mixed)
    if n == 4:
        others = [shifted(hidden, 1), shifted(hidden, -1), shifted(hidden, 2)]
    else:
        others = [lax.all_gather(hidden, "rows")]
    decoded = call(attention, struct((plane, channels)))(
        hidden,
        *others,
        third_gain.reshape(1, -1),
        third_shift.reshape(1, -1),
        query_weight,
        key_weight,
        value_weight,
        output_weight,
    )
    return decoded.reshape(features.shape)


def solution(mesh):
    in_specs = (
        P(("clips", "tm"), "rows", None, None),
        P(),
        P(),
        P("tm", None, None, None, None),
        P("tm"),
        P(),
        P(),
        P("tm", None, None, None, None),
        P("tm"),
        P(),
        P(),
        P(),
        P(),
        P(),
        P(),
    )
    out_specs = P(("clips", "tm"), "rows", None, None)
    return jax.shard_map(
        per_device, mesh=mesh, in_specs=in_specs, out_specs=out_specs, check_vma=False
    )
```

time: 158 us -> 62.1 us (0.39)
  blocking collectives: 116 us -> 22.3 us
  matrix products: 9.27 us -> 0 us
  Pallas kernels: 0 us -> 7.82 us
  waiting for transfers between devices: 3.52 us -> 10.7 us
  local copies, waits for them, and re-layouts: 12.1 us -> 6.17 us
  other arithmetic: 5.53 us -> 0 us
  starting transfers between devices: 10.1 us -> 14.6 us
    psum x6 -> x0, blocking collectives: 59.3 us -> none  [the longest x3 32.1 us: group_norm(): sums = lax.psum(jnp.sum(grouped, axis=(1, 2, 4)), 'rows')]
    all_gather x4 -> x2, blocking collectives: 43.1 us -> 15.6 us  [the longest x1 7.89 us: per_device(): parts = lax.all_gather(active2, 'tm')]
    dot_general x23 -> x0, matrix products: 9.27 us -> none  [the longest x18 7.32 us: causal_conv(): lax.dot_general(tap_weight, stacked.reshape(-1, 3 * channels), (((1,), (1...]
    slice x26 -> x0, local copies, waits for them, and re-layouts: 8.99 us -> none  [the longest x20 4.78 us: causal_conv(): tap_weight = kernel[:, tap_time, tap_row].reshape(outputs, 3 * channels)]
    pallas_call x0 -> x7, Pallas kernels: none -> 7.82 us  [run(): pl.pallas_call(body, out_shape=outs, in_specs=[SMEM if a.dtype == jnp.int...]
    ppermute x4 -> x9, waiting for transfers between devices: 3.52 us -> 10.7 us  [shifted(): lax.ppermute(value, 'rows', [(i, (i + by) % count) for i in range(count)])]
    all_to_all x2 -> x1, blocking collectives: 13.4 us -> 6.74 us  [per_device(): mixed = lax.all_to_all(conv2, 'tm', split_axis=0, concat_axis=0, tiled=True)]
    ppermute x4 -> x9, starting transfers between devices: 10.1 us -> 14.6 us  [shifted(): lax.ppermute(value, 'rows', [(i, (i + by) % count) for i in range(count)])]
  transfers between devices with their start and end apart: 4 -> 9, of which waited for: 2 -> 5; matrix products, arithmetic and copies ran while one was open for 3% -> 3% of each run, Pallas kernels for 0% -> 0%
where the time goes in v1:
time: 62.1 us; the launch traced here: 61.7 us
  blocking collectives  22.3 us (36%)
  starting transfers between devices  14.6 us (24%)
  waiting for transfers between devices  10.7 us (17%)
  Pallas kernels  7.82 us (13%)
  local copies, waits for them, and re-layouts  6.17 us (10%)
    ppermute x9, starting transfers between devices, shifted(): lax.ppermute(value, 'rows', [(i, (i + by) % count) for i in range(count)])  14.6 us
    ppermute x9, waiting for transfers between devices, shifted(): lax.ppermute(value, 'rows', [(i, (i + by) % count) for i in range(count)])  10.7 us
    all_gather x1, blocking collectives, per_device(): parts = lax.all_gather(active2, 'tm')  7.89 us
    pallas_call x7, Pallas kernels, run(): pl.pallas_call(body, out_shape=outs, in_specs=[SMEM if a.dtype == jnp.int...  7.82 us
    all_gather x1, blocking collectives, per_device(): clip = lax.all_gather(active1, 'tm', axis=0, tiled=True)  7.68 us
    all_to_all x1, blocking collectives, per_device(): mixed = lax.all_to_all(conv2, 'tm', split_axis=0, concat_axis=0, tiled=True)  6.74 us
    unnamed x26, local copies, waits for them, and re-layouts  4.03 us
  transfers between devices with their start and end apart: 9, of which 5 were waited for; matrix products, arithmetic and copies ran while one was open for 3% of the time, Pallas kernels for 0%

profile of v1, /device:TPU:0, one launch (start us, length us, event | category | flops | bytes accessed | tf_op | source)
XLA Modules:
  0.0 61.7 jit_solution(10658703439091513687)
XLA Ops:
  0.0 0.9 %copy-done.2 = bf16[1,2,48,384]{3,2,1,0:T(8,128)(2,1)S(1)} copy-done((bf16[1,2,48,384]{3,2,1,0:T(8,128)(2,1)S(1)}, bf16[1,2,48,384]{3,2,1,0:T(8,128)(2,1)}, u32[]{:S(2)}) %copy-start.2) | copy-done | bytes 73752
  0.9 0.9 %shard_map.145 = (bf16[64,384]{1,0:T(8,128)(2,1)S(1)}, bf16[64,384]{1,0:T(8,128)(2,1)S(1)}, bf16[16,384]{1,0:T(8,128)(2,1)S(1)}) custom-call(bf16[1,2,48,384]{3,2,1,0:T(8,128)(2,1)S(1)} %copy-done.2), custom_call_target="tpu_custom_call" | custom-call | tf_op jit(solution)/shard_map/pallas_call | solution.py:22
  1.8 3.1 %collective-permute-start = (bf16[64,384]{1,0:T(8,128)(2,1)S(1)}, bf16[64,384]{1,0:T(8,128)(2,1)S(1)}, u32[]{:S(2)}, u32[]{:S(2)}) collective-permute-start(bf16[64,384]{1,0:T(8,128)(2,1)S(1)} %get-tuple-element.12), channel_id=1, source_target_pairs={{0,1},{1,2},{2,3},{3,0},{4,5},{5,6},{6,7},{7,4},{8,9},{9,10},{10,1... | collective-permute-start | bytes 147464 | tf_op jit(solution)/shard_map/ppermute | solution.py:241
  4.9 2.1 %collective-permute-start.1 = (bf16[64,384]{1,0:T(8,128)(2,1)S(1)}, bf16[64,384]{1,0:T(8,128)(2,1)S(1)}, u32[]{:S(2)}, u32[]{:S(2)}) collective-permute-start(bf16[64,384]{1,0:T(8,128)(2,1)S(1)} %get-tuple-element.13), channel_id=1, source_target_pairs={{0,3},{1,0},{2,1},{3,2},{4,7},{5,4},{6,5},{7,6},{8,11},{9,8},{10,9... | collective-permute-start | bytes 147464 | tf_op jit(solution)/shard_map/ppermute | solution.py:241
  7.0 0.9 %collective-permute-start.2 = (bf16[16,384]{1,0:T(8,128)(2,1)S(1)}, bf16[16,384]{1,0:T(8,128)(2,1)S(1)}, u32[]{:S(2)}, u32[]{:S(2)}) collective-permute-start(bf16[16,384]{1,0:T(8,128)(2,1)S(1)} %get-tuple-element.14.own_ref), channel_id=1, source_target_pairs={{0,2},{1,3},{2,0},{3,1},{4,6},{5,7},{6,4},{7,5},{8,10},{9,11},{10,... | collective-permute-start | bytes 36872 | tf_op jit(solution)/shard_map/ppermute | solution.py:241
  7.9 0.7 %reshape.37.gain_ref = f32[1,384]{1,0:T(1,128)S(1)} reshape(f32[384]{0:T(512)} %param.16) | data formatting | bytes 3072 | tf_op jit(solution)/shard_map/reshape | solution.py:282
  8.6 0.7 %reshape.38.shift_ref = f32[1,384]{1,0:T(1,128)S(1)} reshape(f32[384]{0:T(512)} %param.17) | data formatting | bytes 3072 | tf_op jit(solution)/shard_map/reshape | solution.py:282
  9.3 2.3 %collective-permute-done.2.others_ref = bf16[16,384]{1,0:T(8,128)(2,1)S(1)} collective-permute-done((bf16[16,384]{1,0:T(8,128)(2,1)S(1)}, bf16[16,384]{1,0:T(8,128)(2,1)S(1)}, u32[]{:S(2)}, u32[]{:S(2)}) %collective-permute-start.2) | collective-permute-done | bytes 12320 | tf_op jit(solution)/shard_map/ppermute | solution.py:241
  11.6 0.0 collective-permute-done.prev_ref
  11.6 0.0 collective-permute-done.1.next_ref
  11.6 0.9 %copy-done.3 = bf16[1,2,48,384]{3,2,1,0:T(8,128)(2,1)S(1)} copy-done((bf16[1,2,48,384]{3,2,1,0:T(8,128)(2,1)S(1)}, bf16[1,2,48,384]{3,2,1,0:T(8,128)(2,1)}, u32[]{:S(2)}) %copy-start.3) | copy-done | bytes 73752
  12.4 0.1 shard_map.146
  12.6 7.7 %all_gather.9.a_ref = bf16[4,4,48,384]{3,2,1,0:T(8,128)(2,1)S(1)} all-gather(bf16[1,4,48,384]{3,2,1,0:T(8,128)(2,1)S(1)} %shard_map.146), channel_id=1, replica_groups=mesh['clips'=2,'tm'=4,'rows'=4] {'tm'}, dimensions={0}, use_global_device_ids=true | all-gather | bytes 737280 | tf_op jit(solution)/shard_map/all_gather | solution.py:284
  20.3 1.6 %copy-done = bf16[96,3,3,3,384]{4,0,3,2,1:T(8,128)(2,1)S(1)} copy-done((bf16[96,3,3,3,384]{4,0,3,2,1:T(8,128)(2,1)S(1)}, bf16[96,3,3,3,384]{4,0,3,2,1:T(8,128)(2,1)}, u32[]{:S(2)}) %copy-start) | copy-done | bytes 1990680
  21.8 0.7 %copy-done.10 = f32[96]{0:T(128)S(1)} copy-done((f32[96]{0:T(128)S(1)}, f32[96]{0:T(128)}, u32[]{:S(2)}) %copy-start.10) | copy-done | bytes 408
  22.5 2.2 %shard_map.147 = (bf16[4,2,48,96]{3,2,1,0:T(8,128)(2,1)S(1)}, bf16[240,96]{1,0:T(8,128)(2,1)S(1)}, bf16[240,96]{1,0:T(8,128)(2,1)S(1)}, bf16[48,96]{1,0:T(8,128)(2,1)S(1)}) custom-call(bf16[4,4,48,384]{3,2,1,0:T(8,128)(2,1)S(1)} %all_gather.9.a_ref, bf16[3,3,288,384]{3,2,1,0:T(8,128)(2,1)S(1)} %bitcast.16, f32[1,96]{1,0:T(1,128)S(1)} %bitcast.19), custom_call_target="tpu_custom_call" | custom-call | tf_op jit(solution)/shard_map/pallas_call | solution.py:22
  24.7 0.8 %collective-permute-start.5 = (bf16[48,96]{1,0:T(8,128)(2,1)S(1)}, bf16[48,96]{1,0:T(8,128)(2,1)S(1)}, u32[]{:S(2)}, u32[]{:S(2)}) collective-permute-start(bf16[48,96]{1,0:T(8,128)(2,1)S(1)} %get-tuple-element.18.own_ref), channel_id=1, source_target_pairs={{0,2},{1,3},{2,0},{3,1},{4,6},{5,7},{6,4},{7,5},{8,10},{9,11},{10,... | collective-permute-start | bytes 27656 | tf_op jit(solution)/shard_map/ppermute | solution.py:241
  25.5 1.6 %collective-permute-start.3 = (bf16[240,96]{1,0:T(8,128)(2,1)S(1)}, bf16[240,96]{1,0:T(8,128)(2,1)S(1)}, u32[]{:S(2)}, u32[]{:S(2)}) collective-permute-start(bf16[240,96]{1,0:T(8,128)(2,1)S(1)} %get-tuple-element.16), channel_id=1, source_target_pairs={{0,1},{1,2},{2,3},{3,0},{4,5},{5,6},{6,7},{7,4},{8,9},{9,10},{10,1... | collective-permute-start | bytes 138248 | tf_op jit(solution)/shard_map/ppermute | solution.py:241
  27.1 2.2 %collective-permute-start.4 = (bf16[240,96]{1,0:T(8,128)(2,1)S(1)}, bf16[240,96]{1,0:T(8,128)(2,1)S(1)}, u32[]{:S(2)}, u32[]{:S(2)}) collective-permute-start(bf16[240,96]{1,0:T(8,128)(2,1)S(1)} %get-tuple-element.17), channel_id=1, source_target_pairs={{0,3},{1,0},{2,1},{3,2},{4,7},{5,4},{6,5},{7,6},{8,11},{9,8},{10,9... | collective-permute-start | bytes 138248 | tf_op jit(solution)/shard_map/ppermute | solution.py:241
  29.3 0.8 %dynamic-slice_bitcast_fusion = (f32[1,96]{1,0:T(1,128)S(1)}, f32[1,96]{1,0:T(1,128)S(1)}) fusion(f32[384]{0:T(512)} %param.21, s32[]{:T(128)S(6)} %select_n.4, f32[384]{0:T(512)} %param.20), kind=kLoop, calls=%fused_computation | loop fusion | bytes 1540 | tf_op jit(solution)/shard_map/reshape | solution.py:303
  30.1 0.0 collective-permute-done.5.others_ref
  30.1 1.9 %collective-permute-done.3.prev_ref = bf16[240,96]{1,0:T(8,128)(2,1)S(1)} collective-permute-done((bf16[240,96]{1,0:T(8,128)(2,1)S(1)}, bf16[240,96]{1,0:T(8,128)(2,1)S(1)}, u32[]{:S(2)}, u32[]{:S(2)}) %collective-permute-start.3) | collective-permute-done | bytes 46112 | tf_op jit(solution)/shard_map/ppermute | solution.py:241
  32.0 0.1 collective-permute-done.4.next_ref
  32.1 0.2 shard_map.148
  32.3 0.0 copy-start.4
  32.3 0.0 copy-start.11
  32.3 0.0 copy-start.12
  32.3 0.0 copy-start.5
  32.3 0.0 copy-start.6
  32.3 0.0 copy-start.7
  32.4 0.0 copy-start.8
  32.4 7.9 %all-gather = bf16[16,4,48,96]{3,2,1,0:T(8,128)(2,1)S(1)} all-gather(bf16[4,4,48,96]{3,2,1,0:T(8,128)(2,1)S(1)} %shard_map.148), channel_id=2, replica_groups=mesh['clips'=2,'tm'=4,'rows'=4] {'tm'}, dimensions={0}, use_global_device_ids=true | all-gather | bytes 737280 | tf_op jit(solution)/shard_map/all_gather | solution.py:305
  40.3 0.0 copy-done.1
  40.3 0.0 copy-done.9
  40.3 1.6 %shard_map.149 = bf16[4,96,96]{2,1,0:T(8,128)(2,1)S(1)} custom-call(bf16[4,4,4,48,96]{4,3,2,1,0:T(8,128)(2,1)S(1)} %bitcast.15, bf16[3,3,288,384]{3,2,1,0:T(8,128)(2,1)S(1)} %bitcast.17, f32[1,96]{1,0:T(1,128)S(1)} %bitcast.18), custom_call_target="tpu_custom_call" | custom-call | tf_op jit(solution)/shard_map/pallas_call | solution.py:22
  41.9 6.7 %all_to_all.5.parts_ref = bf16[4,96,96]{2,1,0:T(8,128)(2,1)S(1)} all-to-all(bf16[4,96,96]{2,1,0:T(8,128)(2,1)S(1)} %shard_map.149), channel_id=1, replica_groups=mesh['clips'=2,'tm'=4,'rows'=4] {'tm'}, dimensions={0} | all-to-all | bytes 147456 | tf_op jit(solution)/shard_map/all_to_all | solution.py:311
  48.6 0.0 copy-done.4
  48.6 0.1 shard_map.150.own_ref
  48.7 1.3 %collective-permute-start.6 = (bf16[96,384]{1,0:T(8,128)(2,1)S(1)}, bf16[96,384]{1,0:T(8,128)(2,1)S(1)}, u32[]{:S(2)}, u32[]{:S(2)}) collective-permute-start(bf16[96,384]{1,0:T(8,128)(2,1)S(1)} %shard_map.150.own_ref), channel_id=1, source_target_pairs={{0,1},{1,2},{2,3},{3,0},{4,5},{5,6},{6,7},{7,4},{8,9},{9,10},{10,1... | collective-permute-start | bytes 221192 | tf_op jit(solution)/shard_map/ppermute | solution.py:241
  50.1 2.5 %collective-permute-start.7 = (bf16[96,384]{1,0:T(8,128)(2,1)S(1)}, bf16[96,384]{1,0:T(8,128)(2,1)S(1)}, u32[]{:S(2)}, u32[]{:S(2)}) collective-permute-start(bf16[96,384]{1,0:T(8,128)(2,1)S(1)} %shard_map.150.own_ref), channel_id=1, source_target_pairs={{0,3},{1,0},{2,1},{3,2},{4,7},{5,4},{6,5},{7,6},{8,11},{9,8},{10,9... | collective-permute-start | bytes 221192 | tf_op jit(solution)/shard_map/ppermute | solution.py:241
  52.6 0.0 collective-permute-start.8
  52.6 0.0 copy-done.11
  52.7 3.2 %collective-permute-done.6.refs_0_ = bf16[96,384]{1,0:T(8,128)(2,1)S(1)} collective-permute-done((bf16[96,384]{1,0:T(8,128)(2,1)S(1)}, bf16[96,384]{1,0:T(8,128)(2,1)S(1)}, u32[]{:S(2)}, u32[]{:S(2)}) %collective-permute-start.6) | collective-permute-done | bytes 73760 | tf_op jit(solution)/shard_map/ppermute | solution.py:241
  55.8 0.0 collective-permute-done.7.refs_1_
  55.8 3.2 %collective-permute-done.8.refs_2_ = bf16[96,384]{1,0:T(8,128)(2,1)S(1)} collective-permute-done((bf16[96,384]{1,0:T(8,128)(2,1)S(1)}, bf16[96,384]{1,0:T(8,128)(2,1)S(1)}, u32[]{:S(2)}, u32[]{:S(2)}) %collective-permute-start.8) | collective-permute-done | bytes 73760 | tf_op jit(solution)/shard_map/ppermute | solution.py:241
  59.0 0.0 copy-done.7
  59.1 0.0 copy-done.8
  59.1 2.7 %shard_map.151 = bf16[96,384]{1,0:T(8,128)(2,1)} custom-call(bf16[96,384]{1,0:T(8,128)(2,1)S(1)} %shard_map.150.own_ref, bf16[96,384]{1,0:T(8,128)(2,1)S(1)} %collective-permute-done.6.refs_0_, bf16[96,384]{1,0:T(8,128)(2,1)S(1)} %collective-permute-done.7.refs_1_, bf16[96,384]{1,0:T(8,128)(2,1)S(1)} %collective-permute-done.8.refs_2_, ...), custom_call_target="tpu_custom_call" | custom-call | tf_op jit(solution)/shard_map/pallas_call | solution.py:22
  (11 shorter events, 0.0 us)
Async XLA Ops:
  0.0 0.9 %copy-start.2 = (bf16[1,2,48,384]{3,2,1,0:T(8,128)(2,1)S(1)}, bf16[1,2,48,384]{3,2,1,0:T(8,128)(2,1)}, u32[]{:S(2)}) copy-start(bf16[1,2,48,384]{3,2,1,0:T(8,128)(2,1)} %x_ref.5) | copy-start | bytes 221188
  1.8 9.8 %collective-permute-start = (bf16[64,384]{1,0:T(8,128)(2,1)S(1)}, bf16[64,384]{1,0:T(8,128)(2,1)S(1)}, u32[]{:S(2)}, u32[]{:S(2)}) collective-permute-start(bf16[64,384]{1,0:T(8,128)(2,1)S(1)} %get-tuple-element.12), channel_id=1, source_target_pairs={{0,1},{1,2},{2,3},{3,0},{4,5},{5,6},{6,7},{7,4},{8,9},{9,10},{10,1... | collective-permute-start | bytes 147464 | tf_op jit(solution)/shard_map/ppermute | solution.py:241
  4.9 6.7 %collective-permute-start.1 = (bf16[64,384]{1,0:T(8,128)(2,1)S(1)}, bf16[64,384]{1,0:T(8,128)(2,1)S(1)}, u32[]{:S(2)}, u32[]{:S(2)}) collective-permute-start(bf16[64,384]{1,0:T(8,128)(2,1)S(1)} %get-tuple-element.13), channel_id=1, source_target_pairs={{0,3},{1,0},{2,1},{3,2},{4,7},{5,4},{6,5},{7,6},{8,11},{9,8},{10,9... | collective-permute-start | bytes 147464 | tf_op jit(solution)/shard_map/ppermute | solution.py:241
  7.0 4.6 %collective-permute-start.2 = (bf16[16,384]{1,0:T(8,128)(2,1)S(1)}, bf16[16,384]{1,0:T(8,128)(2,1)S(1)}, u32[]{:S(2)}, u32[]{:S(2)}) collective-permute-start(bf16[16,384]{1,0:T(8,128)(2,1)S(1)} %get-tuple-element.14.own_ref), channel_id=1, source_target_pairs={{0,2},{1,3},{2,0},{3,1},{4,6},{5,7},{6,4},{7,5},{8,10},{9,11},{10,... | collective-permute-start | bytes 36872 | tf_op jit(solution)/shard_map/ppermute | solution.py:241
  11.6 0.9 %copy-start.3 = (bf16[1,2,48,384]{3,2,1,0:T(8,128)(2,1)S(1)}, bf16[1,2,48,384]{3,2,1,0:T(8,128)(2,1)}, u32[]{:S(2)}) copy-start(bf16[1,2,48,384]{3,2,1,0:T(8,128)(2,1)} %x_ref.5) | copy-start | bytes 221188
  20.3 1.6 %copy-start = (bf16[96,3,3,3,384]{4,0,3,2,1:T(8,128)(2,1)S(1)}, bf16[96,3,3,3,384]{4,0,3,2,1:T(8,128)(2,1)}, u32[]{:S(2)}) copy-start(bf16[96,3,3,3,384]{4,0,3,2,1:T(8,128)(2,1)} %param.18) | copy-start | bytes 5971972
  21.8 0.7 %copy-start.10 = (f32[96]{0:T(128)S(1)}, f32[96]{0:T(128)}, u32[]{:S(2)}) copy-start(f32[96]{0:T(128)} %param.19) | copy-start | bytes 1156
  22.5 17.8 %copy-start.1 = (bf16[96,3,3,3,384]{4,0,3,2,1:T(8,128)(2,1)S(1)}, bf16[96,3,3,3,384]{4,0,3,2,1:T(8,128)(2,1)}, u32[]{:S(2)}) copy-start(bf16[96,3,3,3,384]{4,0,3,2,1:T(8,128)(2,1)} %param.22) | copy-start | bytes 5971972
  22.5 17.8 %copy-start.9 = (f32[96]{0:T(128)S(1)}, f32[96]{0:T(128)}, u32[]{:S(2)}) copy-start(f32[96]{0:T(128)} %param.23) | copy-start | bytes 1156
  24.7 5.4 %collective-permute-start.5 = (bf16[48,96]{1,0:T(8,128)(2,1)S(1)}, bf16[48,96]{1,0:T(8,128)(2,1)S(1)}, u32[]{:S(2)}, u32[]{:S(2)}) collective-permute-start(bf16[48,96]{1,0:T(8,128)(2,1)S(1)} %get-tuple-element.18.own_ref), channel_id=1, source_target_pairs={{0,2},{1,3},{2,0},{3,1},{4,6},{5,7},{6,4},{7,5},{8,10},{9,11},{10,... | collective-permute-start | bytes 27656 | tf_op jit(solution)/shard_map/ppermute | solution.py:241
  25.5 6.5 %collective-permute-start.3 = (bf16[240,96]{1,0:T(8,128)(2,1)S(1)}, bf16[240,96]{1,0:T(8,128)(2,1)S(1)}, u32[]{:S(2)}, u32[]{:S(2)}) collective-permute-start(bf16[240,96]{1,0:T(8,128)(2,1)S(1)} %get-tuple-element.16), channel_id=1, source_target_pairs={{0,1},{1,2},{2,3},{3,0},{4,5},{5,6},{6,7},{7,4},{8,9},{9,10},{10,1... | collective-permute-start | bytes 138248 | tf_op jit(solution)/shard_map/ppermute | solution.py:241
  27.1 5.0 %collective-permute-start.4 = (bf16[240,96]{1,0:T(8,128)(2,1)S(1)}, bf16[240,96]{1,0:T(8,128)(2,1)S(1)}, u32[]{:S(2)}, u32[]{:S(2)}) collective-permute-start(bf16[240,96]{1,0:T(8,128)(2,1)S(1)} %get-tuple-element.17), channel_id=1, source_target_pairs={{0,3},{1,0},{2,1},{3,2},{4,7},{5,4},{6,5},{7,6},{8,11},{9,8},{10,9... | collective-permute-start | bytes 138248 | tf_op jit(solution)/shard_map/ppermute | solution.py:241
  32.3 16.4 %copy-start.4 = (bf16[1,2,48,384]{3,2,1,0:T(8,128)(2,1)S(1)}, bf16[1,2,48,384]{3,2,1,0:T(8,128)(2,1)}, u32[]{:S(2)}) copy-start(bf16[1,2,48,384]{3,2,1,0:T(8,128)(2,1)} %x_ref.5) | copy-start | bytes 221188
  32.3 20.3 %copy-start.11 = (f32[384]{0:T(512)S(1)}, f32[384]{0:T(512)}, u32[]{:S(2)}) copy-start(f32[384]{0:T(512)} %param.24) | copy-start | bytes 4612
  32.3 20.3 %copy-start.12 = (f32[384]{0:T(512)S(1)}, f32[384]{0:T(512)}, u32[]{:S(2)}) copy-start(f32[384]{0:T(512)} %param.25) | copy-start | bytes 4612
  32.3 26.7 %copy-start.5 = (bf16[384,384]{1,0:T(8,128)(2,1)S(1)}, bf16[384,384]{1,0:T(8,128)(2,1)}, u32[]{:S(2)}) copy-start(bf16[384,384]{1,0:T(8,128)(2,1)} %refs_5_.1) | copy-start | bytes 884740
  32.3 26.7 %copy-start.6 = (bf16[384,384]{1,0:T(8,128)(2,1)S(1)}, bf16[384,384]{1,0:T(8,128)(2,1)}, u32[]{:S(2)}) copy-start(bf16[384,384]{1,0:T(8,128)(2,1)} %refs_6_.1) | copy-start | bytes 884740
  32.3 26.7 %copy-start.7 = (bf16[384,384]{1,0:T(8,128)(2,1)S(1)}, bf16[384,384]{1,0:T(8,128)(2,1)}, u32[]{:S(2)}) copy-start(bf16[384,384]{1,0:T(8,128)(2,1)} %refs_7_.1) | copy-start | bytes 884740
  32.4 26.7 %copy-start.8 = (bf16[384,384]{1,0:T(8,128)(2,1)S(1)}, bf16[384,384]{1,0:T(8,128)(2,1)}, u32[]{:S(2)}) copy-start(bf16[384,384]{1,0:T(8,128)(2,1)} %refs_8_.1) | copy-start | bytes 884740
  48.7 7.1 %collective-permute-start.6 = (bf16[96,384]{1,0:T(8,128)(2,1)S(1)}, bf16[96,384]{1,0:T(8,128)(2,1)S(1)}, u32[]{:S(2)}, u32[]{:S(2)}) collective-permute-start(bf16[96,384]{1,0:T(8,128)(2,1)S(1)} %shard_map.150.own_ref), channel_id=1, source_target_pairs={{0,1},{1,2},{2,3},{3,0},{4,5},{5,6},{6,7},{7,4},{8,9},{9,10},{10,1... | collective-permute-start | bytes 221192 | tf_op jit(solution)/shard_map/ppermute | solution.py:241
  50.1 5.8 %collective-permute-start.7 = (bf16[96,384]{1,0:T(8,128)(2,1)S(1)}, bf16[96,384]{1,0:T(8,128)(2,1)S(1)}, u32[]{:S(2)}, u32[]{:S(2)}) collective-permute-start(bf16[96,384]{1,0:T(8,128)(2,1)S(1)} %shard_map.150.own_ref), channel_id=1, source_target_pairs={{0,3},{1,0},{2,1},{3,2},{4,7},{5,4},{6,5},{7,6},{8,11},{9,8},{10,9... | collective-permute-start | bytes 221192 | tf_op jit(solution)/shard_map/ppermute | solution.py:241
  52.6 6.4 %collective-permute-start.8 = (bf16[96,384]{1,0:T(8,128)(2,1)S(1)}, bf16[96,384]{1,0:T(8,128)(2,1)S(1)}, u32[]{:S(2)}, u32[]{:S(2)}) collective-permute-start(bf16[96,384]{1,0:T(8,128)(2,1)S(1)} %shard_map.150.own_ref), channel_id=1, source_target_pairs={{0,2},{1,3},{2,0},{3,1},{4,6},{5,7},{6,4},{7,5},{8,10},{9,11},{10,... | collective-permute-start | bytes 221192 | tf_op jit(solution)/shard_map/ppermute | solution.py:241

commit v2 on v1

--- a/solution.py
+++ b/solution.py
@@ -25,7 +25,7 @@
             in_specs=[SMEM if a.dtype == jnp.int32 else VMEM for a in args],
             out_specs=jax.tree.map(lambda _: VMEM, outs),
             scratch_shapes=scratch,
-            compiler_params=pltpu.CompilerParams(vmem_limit_bytes=40 * 1024 * 1024),
+            compiler_params=pltpu.CompilerParams(vmem_limit_bytes=24 * 1024 * 1024),
             **kwargs,
         )(*args)
 
@@ -41,13 +41,10 @@
     first = lax.broadcasted_iota(jnp.int32, (channels, channels), 0)
     second = lax.broadcasted_iota(jnp.int32, (channels, channels), 1)
     same = ((first * 43691) >> 19) == ((second * 43691) >> 19)
-    return lax.dot_general(
-        rows,
-        same.astype(F32),
-        (((1,), (0,)), ((), ())),
-        precision=lax.Precision.HIGHEST,
-        preferred_element_type=F32,
-    )
+    terms = jnp.concatenate(split3(rows), axis=0).astype(BF16)
+    sums = jnp.dot(terms, same.astype(BF16), preferred_element_type=F32)
+    size = rows.shape[0]
+    return sums[0:size] + sums[size : 2 * size] + sums[2 * size :]
 
 
 def split3(value):
@@ -137,6 +134,36 @@
     return (result + bias).astype(BF16)
 
 
+def clip_norm(r, x_ref, gain, shift, a_ref, rows8):
+    frames, height, cols, channels = x_ref.shape
+    _, padded, _, _ = a_ref.shape
+    rows = padded - 2
+    count = height * cols * GROUP
+    rows8[...] = jnp.zeros(rows8.shape, F32)
+    for f in range(frames):
+        wide = x_ref[f].astype(F32).reshape(height * cols, channels)
+        rows8[f : f + 1] = jnp.sum(wide, axis=0, keepdims=True)
+    mean = group_sums(rows8[...]) / count
+    for f in range(frames):
+        wide = x_ref[f].astype(F32).reshape(height * cols, channels)
+        rows8[f : f + 1] = jnp.sum(jnp.square(wide - mean[f : f + 1]), axis=0, keepdims=True)
+    variance = group_sums(rows8[...]) / count
+    scale = lax.rsqrt(variance + EPSILON) * gain
+    for row in range(padded):
+        at = r * rows + row - 1
+        inside = jnp.logical_and(at >= 0, at < height)
+        at = jnp.clip(at, 0, height - 1)
+        for f in range(frames):
+            value = silu((x_ref[f, at].astype(F32) - mean[f : f + 1]) * scale[f : f + 1] + shift)
+            a_ref[f, row] = jnp.where(inside, value, 0.0).astype(BF16)
+
+
+def first_conv_clip(r_ref, x_ref, gain_ref, shift_ref, w_ref, bias_ref, *refs):
+    outs, (a_ref, rows8, wide8) = refs[:-3], refs[-3:]
+    clip_norm(r_ref[0], x_ref, gain_ref[...], shift_ref[...], a_ref, wide8)
+    first_conv(a_ref, w_ref, bias_ref, *outs, rows8)
+
+
 def first_conv(a_ref, w_ref, bias_ref, out_ref, down_ref, up_ref, own_ref, rows8):
     frames, padded, cols, channels = a_ref.shape
     rows = padded - 2
@@ -275,22 +302,33 @@
     def taps(kernel):
         return jnp.transpose(kernel, (1, 2, 3, 0, 4)).reshape(3, 3, 3 * outputs, channels)
 
-    message = struct((cols + 16, channels))
-    down, up, own = call(first_stats, (message, message, struct((16, channels))))(features)
-    prev, after, others = around(down, up, own)
-    active1 = call(functools.partial(first_norm, n), struct((1, rows + 2, cols, channels)))(
-        r, features, prev, after, own, others, first_gain.reshape(1, -1), first_shift.reshape(1, -1)
-    )
-    clip = lax.all_gather(active1, "tm", axis=0, tiled=True)
-
     step = 8 * (-(-frames // 8))
     size = 6 * step
     message = struct((frames * cols + size, outputs))
-    conv1, down, up, own = call(
-        first_conv,
-        (struct((frames, rows, cols, outputs)), message, message, struct((size, outputs))),
-        (pltpu.VMEM((step, outputs), F32),),
-    )(clip, taps(first_kernel), first_bias.reshape(1, -1))
+    conv1_outs = (struct((frames, rows, cols, outputs)), message, message, struct((size, outputs)))
+    if n == 4:
+        clip = lax.all_gather(features, ("tm", "rows"))
+        clip = clip.reshape(frames, n * rows, cols, channels)
+        conv1, down, up, own = call(
+            first_conv_clip,
+            conv1_outs,
+            (
+                pltpu.VMEM((frames, rows + 2, cols, channels), BF16),
+                pltpu.VMEM((step, outputs), F32),
+                pltpu.VMEM((step, channels), F32),
+            ),
+        )(r, clip, first_gain.reshape(1, -1), first_shift.reshape(1, -1), taps(first_kernel), first_bias.reshape(1, -1))
+    else:
+        narrow = struct((cols + 16, channels))
+        down, up, own = call(first_stats, (narrow, narrow, struct((16, channels))))(features)
+        prev, after, others = around(down, up, own)
+        active1 = call(functools.partial(first_norm, n), struct((1, rows + 2, cols, channels)))(
+            r, features, prev, after, own, others, first_gain.reshape(1, -1), first_shift.reshape(1, -1)
+        )
+        clip = lax.all_gather(active1, "tm", axis=0, tiled=True)
+        conv1, down, up, own = call(first_conv, conv1_outs, (pltpu.VMEM((step, outputs), F32),))(
+            clip, taps(first_kernel), first_bias.reshape(1, -1)
+        )
     prev, after, others = around(down, up, own)
     active2 = call(functools.partial(second_norm, n), struct((frames, rows + 2, cols, outputs)))(
         r,

time: 62.1 us -> 101 us (1.63)
  waiting for transfers between devices: 10.7 us -> 52.3 us
  between operations: 0.14 us -> 13.5 us
  blocking collectives: 22.3 us -> 14.6 us
  starting transfers between devices: 14.6 us -> 7.75 us
    all_gather x0 -> x1, waiting for transfers between devices: none -> 42.1 us  [per_device(): clip = lax.all_gather(features, ('tm', 'rows'))]
    all_gather x1 -> x0, blocking collectives: 7.68 us -> none  [per_device(): clip = lax.all_gather(active1, 'tm', axis=0, tiled=True)]
    ppermute x9 -> x6, starting transfers between devices: 14.6 us -> 7.74 us  [shifted(): lax.ppermute(value, 'rows', [(i, (i + by) % count) for i in range(count)])]
    ppermute x9 -> x6, waiting for transfers between devices: 10.7 us -> 9.44 us  [shifted(): lax.ppermute(value, 'rows', [(i, (i + by) % count) for i in range(count)])]
    unnamed x26 -> x24, local copies, waits for them, and re-layouts: 4.03 us -> 3.53 us
    pallas_call x7 -> x5, Pallas kernels: 7.82 us -> 7.34 us  [run(): pl.pallas_call(body, out_shape=outs, in_specs=[SMEM if a.dtype == jnp.int...]
  transfers between devices with their start and end apart: 9 -> 7, of which waited for: 5 -> 4; matrix products, arithmetic and copies ran while one was open for 3% -> 2% of each run, Pallas kernels for 0% -> 0%
where the time goes in v2:
time: 101 us
  waiting for transfers between devices  52.3 us (52%)
  blocking collectives  14.6 us (14%)
  between operations  13.5 us (13%)
  starting transfers between devices  7.75 us (8%)
  Pallas kernels  7.34 us (7%)
  local copies, waits for them, and re-layouts  5.67 us (6%)
    all_gather x1, waiting for transfers between devices, per_device(): clip = lax.all_gather(features, ('tm', 'rows'))  42.1 us
    ppermute x6, waiting for transfers between devices, shifted(): lax.ppermute(value, 'rows', [(i, (i + by) % count) for i in range(count)])  9.44 us
    all_gather x1, blocking collectives, per_device(): parts = lax.all_gather(active2, 'tm')  7.97 us
    ppermute x6, starting transfers between devices, shifted(): lax.ppermute(value, 'rows', [(i, (i + by) % count) for i in range(count)])  7.74 us
    pallas_call x5, Pallas kernels, run(): pl.pallas_call(body, out_shape=outs, in_specs=[SMEM if a.dtype == jnp.int...  7.34 us
    all_to_all x1, blocking collectives, per_device(): mixed = lax.all_to_all(conv2, 'tm', split_axis=0, concat_axis=0, tiled=True)  6.67 us
    unnamed x24, local copies, waits for them, and re-layouts  3.53 us
  transfers between devices with their start and end apart: 7, of which 4 were waited for; matrix products, arithmetic and copies ran while one was open for 2% of the time, Pallas kernels for 0%

profile of v2, /device:TPU:0, one launch (start us, length us, event | category | flops | bytes accessed | tf_op | source)
XLA Modules:
  0.0 101.2 jit_solution(4369163614298290269)
XLA Ops:
  6.5 0.0 all-gather.4.cloned.1.call-start
  6.5 0.7 all-gather.4.cloned.1.call-update
  7.3 0.7 reshape.41.gain_ref
  7.9 0.7 reshape.42.shift_ref
  8.6 42.1 %all-gather.4.cloned.1.call-done = bf16[16,2,48,384]{3,2,1,0:T(8,128)(2,1)} async-done(((bf16[1,2,48,384]{3,2,1,0:T(8,128)(2,1)}), bf16[16,2,48,384]{3,2,1,0:T(8,128)(2,1)}) %all-gather.4.cloned.1.call-update) | async-done | bytes 1179664 | tf_op jit(solution)/shard_map/all_gather | solution.py:310
  50.7 0.0 copy-start
  50.7 1.6 %copy-done = bf16[96,3,3,3,384]{4,0,3,2,1:T(8,128)(2,1)S(1)} copy-done((bf16[96,3,3,3,384]{4,0,3,2,1:T(8,128)(2,1)S(1)}, bf16[96,3,3,3,384]{4,0,3,2,1:T(8,128)(2,1)}, u32[]{:S(2)}) %copy-start) | copy-done | bytes 1990680
  52.3 0.0 copy-start.2
  52.3 1.3 %copy-done.2 = bf16[16,2,48,384]{3,2,1,0:T(8,128)(2,1)S(1)} copy-done((bf16[16,2,48,384]{3,2,1,0:T(8,128)(2,1)S(1)}, bf16[16,2,48,384]{3,2,1,0:T(8,128)(2,1)}, u32[]{:S(2)}) %copy-start.2) | copy-done | bytes 1179672
  53.6 0.0 copy-start.8
  53.6 0.7 copy-done.8
  54.2 0.0 copy-start.1
  54.2 3.3 %shard_map.145 = (bf16[4,2,48,96]{3,2,1,0:T(8,128)(2,1)S(1)}, bf16[240,96]{1,0:T(8,128)(2,1)S(1)}, bf16[240,96]{1,0:T(8,128)(2,1)S(1)}, bf16[48,96]{1,0:T(8,128)(2,1)S(1)}) custom-call(s32[1]{0:T(128)} %bitcast.r_ref, bf16[4,8,48,384]{3,2,1,0:T(8,128)(2,1)S(1)} %bitcast.19, f32[1,384]{1,0:T(1,128)S(1)} %reshape.41.gain_ref, f32[1,384]{1,0:T(1,128)S(1)} %reshape.42.shift_ref, ...), custom_call_target="tpu_custom_call" | custom-call | tf_op jit(solution)/shard_map/pallas_call | solution.py:22
  57.5 0.6 collective-permute-start
  58.1 3.3 %collective-permute-start.1 = (bf16[240,96]{1,0:T(8,128)(2,1)S(1)}, bf16[240,96]{1,0:T(8,128)(2,1)S(1)}, u32[]{:S(2)}, u32[]{:S(2)}) collective-permute-start(bf16[240,96]{1,0:T(8,128)(2,1)S(1)} %get-tuple-element.11), channel_id=1, source_target_pairs={{0,3},{1,0},{2,1},{3,2},{4,7},{5,4},{6,5},{7,6},{8,11},{9,8},{10,9... | collective-permute-start | bytes 138248 | tf_op jit(solution)/shard_map/ppermute | solution.py:268
  61.3 0.0 collective-permute-start.2
  61.3 0.8 dynamic-slice_bitcast_fusion
  62.1 3.8 %collective-permute-done.2.others_ref = bf16[48,96]{1,0:T(8,128)(2,1)S(1)} collective-permute-done((bf16[48,96]{1,0:T(8,128)(2,1)S(1)}, bf16[48,96]{1,0:T(8,128)(2,1)S(1)}, u32[]{:S(2)}, u32[]{:S(2)}) %collective-permute-start.2) | collective-permute-done | bytes 9248 | tf_op jit(solution)/shard_map/ppermute | solution.py:268
  65.9 0.0 collective-permute-done.prev_ref
  65.9 0.0 collective-permute-done.1.next_ref
  65.9 0.2 shard_map.146
  66.1 0.0 copy-start.3
  66.1 0.0 copy-start.10
  66.1 0.0 copy-start.11
  66.2 0.0 copy-start.4
  66.2 0.0 copy-start.5
  66.2 0.0 copy-start.6
  66.2 0.0 copy-start.7
  66.2 8.0 %all-gather.1 = bf16[16,4,48,96]{3,2,1,0:T(8,128)(2,1)S(1)} all-gather(bf16[4,4,48,96]{3,2,1,0:T(8,128)(2,1)S(1)} %shard_map.146), channel_id=3, replica_groups=mesh['clips'=2,'tm'=4,'rows'=4] {'tm'}, dimensions={0}, use_global_device_ids=true | all-gather | bytes 737280 | tf_op jit(solution)/shard_map/all_gather | solution.py:343
  74.2 0.0 copy-done.1
  74.2 0.0 copy-done.9
  74.2 1.6 %shard_map.147 = bf16[4,96,96]{2,1,0:T(8,128)(2,1)S(1)} custom-call(bf16[4,4,4,48,96]{4,3,2,1,0:T(8,128)(2,1)S(1)} %bitcast.16, bf16[3,3,288,384]{3,2,1,0:T(8,128)(2,1)S(1)} %bitcast.18, f32[1,96]{1,0:T(1,128)S(1)} %bitcast.21), custom_call_target="tpu_custom_call" | custom-call | tf_op jit(solution)/shard_map/pallas_call | solution.py:22
  75.8 6.7 %all_to_all.5.parts_ref = bf16[4,96,96]{2,1,0:T(8,128)(2,1)S(1)} all-to-all(bf16[4,96,96]{2,1,0:T(8,128)(2,1)S(1)} %shard_map.147), channel_id=1, replica_groups=mesh['clips'=2,'tm'=4,'rows'=4] {'tm'}, dimensions={0} | all-to-all | bytes 147456 | tf_op jit(solution)/shard_map/all_to_all | solution.py:349
  82.5 0.0 copy-done.3
  82.5 0.1 shard_map.148.own_ref
  82.6 0.1 collective-permute-start.3
  82.7 3.8 %collective-permute-start.4 = (bf16[96,384]{1,0:T(8,128)(2,1)S(1)}, bf16[96,384]{1,0:T(8,128)(2,1)S(1)}, u32[]{:S(2)}, u32[]{:S(2)}) collective-permute-start(bf16[96,384]{1,0:T(8,128)(2,1)S(1)} %shard_map.148.own_ref), channel_id=1, source_target_pairs={{0,3},{1,0},{2,1},{3,2},{4,7},{5,4},{6,5},{7,6},{8,11},{9,8},{10,9... | collective-permute-start | bytes 221192 | tf_op jit(solution)/shard_map/ppermute | solution.py:268
  86.5 0.0 collective-permute-start.5
  86.5 0.0 copy-done.10
  86.5 0.0 copy-done.11
  86.5 3.2 %collective-permute-done.3.refs_0_ = bf16[96,384]{1,0:T(8,128)(2,1)S(1)} collective-permute-done((bf16[96,384]{1,0:T(8,128)(2,1)S(1)}, bf16[96,384]{1,0:T(8,128)(2,1)S(1)}, u32[]{:S(2)}, u32[]{:S(2)}) %collective-permute-start.3) | collective-permute-done | bytes 73760 | tf_op jit(solution)/shard_map/ppermute | solution.py:268
  89.7 0.0 collective-permute-done.4.refs_1_
  89.7 2.4 %collective-permute-done.5.refs_2_ = bf16[96,384]{1,0:T(8,128)(2,1)S(1)} collective-permute-done((bf16[96,384]{1,0:T(8,128)(2,1)S(1)}, bf16[96,384]{1,0:T(8,128)(2,1)S(1)}, u32[]{:S(2)}, u32[]{:S(2)}) %collective-permute-start.5) | collective-permute-done | bytes 73760 | tf_op jit(solution)/shard_map/ppermute | solution.py:268
  92.1 0.0 copy-done.4
  92.1 0.0 copy-done.5
  92.1 0.0 copy-done.6
  92.1 0.0 copy-done.7
  92.1 2.2 %shard_map.149 = bf16[96,384]{1,0:T(8,128)(2,1)} custom-call(bf16[96,384]{1,0:T(8,128)(2,1)S(1)} %shard_map.148.own_ref, bf16[96,384]{1,0:T(8,128)(2,1)S(1)} %collective-permute-done.3.refs_0_, bf16[96,384]{1,0:T(8,128)(2,1)S(1)} %collective-permute-done.4.refs_1_, bf16[96,384]{1,0:T(8,128)(2,1)S(1)} %collective-permute-done.5.refs_2_, ...), custom_call_target="tpu_custom_call" | custom-call | tf_op jit(solution)/shard_map/pallas_call | solution.py:22
  (3 shorter events, 0.0 us)
Async XLA Ops:
  6.5 44.2 %all-gather.4.cloned.1.call-start = ((), (), s32[]{:S(2)}) async-start(), calls=%async_computation.1 | async-start | bytes 1253376 | tf_op jit(solution)/shard_map/all_gather | solution.py:310
  50.7 1.6 %copy-start = (bf16[96,3,3,3,384]{4,0,3,2,1:T(8,128)(2,1)S(1)}, bf16[96,3,3,3,384]{4,0,3,2,1:T(8,128)(2,1)}, u32[]{:S(2)}) copy-start(bf16[96,3,3,3,384]{4,0,3,2,1:T(8,128)(2,1)} %param.18) | copy-start | bytes 5971972
  52.3 1.3 %copy-start.2 = (bf16[16,2,48,384]{3,2,1,0:T(8,128)(2,1)S(1)}, bf16[16,2,48,384]{3,2,1,0:T(8,128)(2,1)}, u32[]{:S(2)}) copy-start(bf16[16,2,48,384]{3,2,1,0:T(8,128)(2,1)} %all-gather.4.cloned.1.call-done) | copy-start | bytes 3538948
  53.6 0.7 copy-start.8
  54.2 20.0 %copy-start.1 = (bf16[96,3,3,3,384]{4,0,3,2,1:T(8,128)(2,1)S(1)}, bf16[96,3,3,3,384]{4,0,3,2,1:T(8,128)(2,1)}, u32[]{:S(2)}) copy-start(bf16[96,3,3,3,384]{4,0,3,2,1:T(8,128)(2,1)} %param.22) | copy-start | bytes 5971972
  54.2 20.0 %copy-start.9 = (f32[96]{0:T(128)S(1)}, f32[96]{0:T(128)}, u32[]{:S(2)}) copy-start(f32[96]{0:T(128)} %param.23) | copy-start | bytes 1156
  57.5 8.5 %collective-permute-start = (bf16[240,96]{1,0:T(8,128)(2,1)S(1)}, bf16[240,96]{1,0:T(8,128)(2,1)S(1)}, u32[]{:S(2)}, u32[]{:S(2)}) collective-permute-start(bf16[240,96]{1,0:T(8,128)(2,1)S(1)} %get-tuple-element.10), channel_id=1, source_target_pairs={{0,1},{1,2},{2,3},{3,0},{4,5},{5,6},{6,7},{7,4},{8,9},{9,10},{10,1... | collective-permute-start | bytes 138248 | tf_op jit(solution)/shard_map/ppermute | solution.py:268
  58.1 7.9 %collective-permute-start.1 = (bf16[240,96]{1,0:T(8,128)(2,1)S(1)}, bf16[240,96]{1,0:T(8,128)(2,1)S(1)}, u32[]{:S(2)}, u32[]{:S(2)}) collective-permute-start(bf16[240,96]{1,0:T(8,128)(2,1)S(1)} %get-tuple-element.11), channel_id=1, source_target_pairs={{0,3},{1,0},{2,1},{3,2},{4,7},{5,4},{6,5},{7,6},{8,11},{9,8},{10,9... | collective-permute-start | bytes 138248 | tf_op jit(solution)/shard_map/ppermute | solution.py:268
  61.3 4.6 %collective-permute-start.2 = (bf16[48,96]{1,0:T(8,128)(2,1)S(1)}, bf16[48,96]{1,0:T(8,128)(2,1)S(1)}, u32[]{:S(2)}, u32[]{:S(2)}) collective-permute-start(bf16[48,96]{1,0:T(8,128)(2,1)S(1)} %get-tuple-element.12.own_ref), channel_id=1, source_target_pairs={{0,2},{1,3},{2,0},{3,1},{4,6},{5,7},{6,4},{7,5},{8,10},{9,11},{10,... | collective-permute-start | bytes 27656 | tf_op jit(solution)/shard_map/ppermute | solution.py:268
  66.1 16.4 %copy-start.3 = (bf16[1,2,48,384]{3,2,1,0:T(8,128)(2,1)S(1)}, bf16[1,2,48,384]{3,2,1,0:T(8,128)(2,1)}, u32[]{:S(2)}) copy-start(bf16[1,2,48,384]{3,2,1,0:T(8,128)(2,1)} %x_ref.1) | copy-start | bytes 221188
  66.1 20.3 %copy-start.10 = (f32[384]{0:T(512)S(1)}, f32[384]{0:T(512)}, u32[]{:S(2)}) copy-start(f32[384]{0:T(512)} %param.24) | copy-start | bytes 4612
  66.1 20.3 %copy-start.11 = (f32[384]{0:T(512)S(1)}, f32[384]{0:T(512)}, u32[]{:S(2)}) copy-start(f32[384]{0:T(512)} %param.25) | copy-start | bytes 4612
  66.2 26.0 %copy-start.4 = (bf16[384,384]{1,0:T(8,128)(2,1)S(1)}, bf16[384,384]{1,0:T(8,128)(2,1)}, u32[]{:S(2)}) copy-start(bf16[384,384]{1,0:T(8,128)(2,1)} %refs_5_.1) | copy-start | bytes 884740
  66.2 26.0 %copy-start.5 = (bf16[384,384]{1,0:T(8,128)(2,1)S(1)}, bf16[384,384]{1,0:T(8,128)(2,1)}, u32[]{:S(2)}) copy-start(bf16[384,384]{1,0:T(8,128)(2,1)} %refs_6_.1) | copy-start | bytes 884740
  66.2 25.9 %copy-start.6 = (bf16[384,384]{1,0:T(8,128)(2,1)S(1)}, bf16[384,384]{1,0:T(8,128)(2,1)}, u32[]{:S(2)}) copy-start(bf16[384,384]{1,0:T(8,128)(2,1)} %refs_7_.1) | copy-start | bytes 884740
  66.2 25.9 %copy-start.7 = (bf16[384,384]{1,0:T(8,128)(2,1)S(1)}, bf16[384,384]{1,0:T(8,128)(2,1)}, u32[]{:S(2)}) copy-start(bf16[384,384]{1,0:T(8,128)(2,1)} %refs_8_.1) | copy-start | bytes 884740
  82.6 7.1 %collective-permute-start.3 = (bf16[96,384]{1,0:T(8,128)(2,1)S(1)}, bf16[96,384]{1,0:T(8,128)(2,1)S(1)}, u32[]{:S(2)}, u32[]{:S(2)}) collective-permute-start(bf16[96,384]{1,0:T(8,128)(2,1)S(1)} %shard_map.148.own_ref), channel_id=1, source_target_pairs={{0,1},{1,2},{2,3},{3,0},{4,5},{5,6},{6,7},{7,4},{8,9},{9,10},{10,1... | collective-permute-start | bytes 221192 | tf_op jit(solution)/shard_map/ppermute | solution.py:268
  82.7 7.1 %collective-permute-start.4 = (bf16[96,384]{1,0:T(8,128)(2,1)S(1)}, bf16[96,384]{1,0:T(8,128)(2,1)S(1)}, u32[]{:S(2)}, u32[]{:S(2)}) collective-permute-start(bf16[96,384]{1,0:T(8,128)(2,1)S(1)} %shard_map.148.own_ref), channel_id=1, source_target_pairs={{0,3},{1,0},{2,1},{3,2},{4,7},{5,4},{6,5},{7,6},{8,11},{9,8},{10,9... | collective-permute-start | bytes 221192 | tf_op jit(solution)/shard_map/ppermute | solution.py:268
  86.5 5.7 %collective-permute-start.5 = (bf16[96,384]{1,0:T(8,128)(2,1)S(1)}, bf16[96,384]{1,0:T(8,128)(2,1)S(1)}, u32[]{:S(2)}, u32[]{:S(2)}) collective-permute-start(bf16[96,384]{1,0:T(8,128)(2,1)S(1)} %shard_map.148.own_ref), channel_id=1, source_target_pairs={{0,2},{1,3},{2,0},{3,1},{4,6},{5,7},{6,4},{7,5},{8,10},{9,11},{10,... | collective-permute-start | bytes 221192 | tf_op jit(solution)/shard_map/ppermute | solution.py:268
Sparse Core Ops, SparseCore 0:
  9.7 41.0 all-gather.3
